TPU v7x, 128 devices: a whole 4x4x4 slice. The times are simulated.
128 devices in a mesh: tm: 8 (over z, x_lo), space: 16 (over x_hi, y, core).
Axes of the slice: x: 4 (x_hi: 2, x_lo: 2; x = x_hi * 2 + x_lo), y: 4, z: 4, core: 2. Of those that a mesh axis runs over, the one named last changes fastest.
Arguments:
- start_states: float32 [8, 128, 16, 1024], P('tm', 'space'), may hold values from 0.2 to 2
- dispersion: float32 [128, 16, 1024], P('space'), may hold values from 0.02 to 0.12
- soil_class: int32 [128, 16, 1024], P('space'), may hold values from 0 to 11
- sorption_k: float32 [12], replicated, may hold values from 0.3 to 3
- sorption_n: float32 [12], replicated, may hold values from 0.6 to 1
Outputs:
- next_states: float32 [8, 128, 16, 1024], P('tm', 'space')
All inputs are finite; a program needn't handle non-finite values.
Results may differ from a plain program's by a relative error of at most 0.0001.
Values sent between devices are 32-bit elements; how exact they have to be, the bound alone decides.
A program may use at most 256 MiB of HBM per device.

v0:
```python
import functools

import jax
import jax.numpy as jnp
from jax import lax
from jax.experimental import pallas as pl
from jax.experimental.pallas import tpu as pltpu
from jax.sharding import PartitionSpec as P

MESH = pl.DeviceIdType.MESH
F32 = jnp.float32

SPEED_X = 0.3
SPEED_Z = 0.2
DENSITY = 2.0

ROWS = 8
HALO = 4
EXT = ROWS + 2 * HALO
NZ = 16
NY = 1024
CROWS = 4
CZ = 8
CY = 512
SLICES = 8
SPACE = 16
HALF = SPACE // 2
GROUPS = HALF + 4
PACKED = GROUPS * CROWS // 2
OWN_PACKED = HALF * CROWS // 2
WINDOWS = 16
LANES = 128

PIECES = (
    (0, 2, 2, 12),
    (1, 3, 1, 12),
    (2, 3, 1, 12),
    (0, 0, 2, 14),
    (1, 2, 1, 13),
    (2, 2, 1, 13),
    (1, 1, 1, 14),
    (2, 1, 1, 14),
)

PLANES = SLICES // 2
PASSES = (1, 2, 4)


def reach(tau):
    return (17 - 2 * tau) // 4


def host_of(half, side):
    return HALF // 2 + (HALF // 2) * half + 2 * side


def shifted(c, axis, size, steps, index):
    rolled = pltpu.roll(c, steps % size, axis)
    return jnp.where(index == (0 if steps > 0 else size - 1), 0.0, rolled)


def update(c, w, e, zm, zp, ym, yp, d, a, m, scale, per_h):
    lap = ((w + e) + (zm + zp)) + ((ym + yp) - 6.0 * c)
    adv = (SPEED_X * per_h) * (c - w) + (SPEED_Z * per_h) * (c - zm)
    ret = 1.0 + a * jnp.exp(m * jnp.log(jnp.abs(c) + 0.1))
    return c + scale * ((d * lap - adv) / ret)


def main_kernel(
    k_in, n_in, start, disp, soil, fine_out, diff_out,
    k_ref, n_ref, u0, u1, u2, dx, cx, ax, mx, rc, rc1, own, dc, ac, mc, drift, win, fwin,
    cbuf, fbuf, cw0, cw1, gout, gbuf,
    local_sem, halo_send, halo_recv, win_send, win_recv, f_send, f_recv, g_send, g_recv, known,
):
    t = lax.axis_index("tm")
    s = lax.axis_index("space")
    core = lax.rem(s, 2)
    half = s // HALF
    is_host = (core == 0) & (s >= host_of(0, 0)) & (s <= host_of(1, 1))
    my_side = lax.rem((s - host_of(0, 0) + SPACE) // 2, 2)
    my_window = t + SLICES * my_side
    is_first = s == 0
    is_last = s == SPACE - 1

    def clear(first):
        for ref in (u0, dx):
            ref[pl.ds(first, HALO)] = jnp.zeros((HALO, NZ, NY), F32)
        cx[pl.ds(first, HALO)] = jnp.zeros((HALO, NZ, NY), jnp.int32)

    plane = t // 2

    def greet(semaphore, distance, planes=0):
        def tell(tt, ss):
            pl.semaphore_signal(semaphore, inc=1, device_id=(tt, ss), device_id_type=MESH)

        @pl.when(s >= distance)
        def _():
            tell(t, s - distance)

        @pl.when(s < SPACE - distance)
        def _():
            tell(t, s + distance)

        if planes:
            tell(t + 1 - 2 * lax.rem(t, 2), s)
            for step in range(1, PLANES):
                there = plane + planes * step

                @pl.when((there >= 0) & (there < PLANES))
                def _():
                    tell(2 * there, s)
                    tell(2 * there + 1, s)

    def greeted(semaphore, distance, planes=0):
        count = (s >= distance).astype(jnp.int32) + (s < SPACE - distance).astype(jnp.int32)
        if planes:
            count = count + 1 + 2 * (plane if planes == 1 else PLANES - 1 - plane)
        pl.semaphore_wait(semaphore, count)

    barrier = pltpu.get_barrier_semaphore()
    greet(barrier, 1, 1)

    local = [
        pltpu.make_async_copy(src, dst.at[pl.ds(HALO, ROWS)], local_sem.at[i])
        for i, (src, dst) in enumerate(((start, u0), (disp, dx), (soil, cx)))
    ]
    local += [
        pltpu.make_async_copy(k_in, k_ref, local_sem.at[3]),
        pltpu.make_async_copy(n_in, n_ref, local_sem.at[4]),
    ]
    for copy in local:
        copy.start()

    @pl.when(is_first)
    def _():
        clear(0)

    @pl.when(is_last)
    def _():
        clear(HALO + ROWS)

    for copy in local:
        copy.wait()

    greeted(barrier, 1, 1)

    targets = (u0, dx, cx)

    def halo_copy(index, side):
        array, low, count, high = PIECES[index]
        first = jnp.where(side == 0, low, high)
        origin = jnp.where(side == 0, low + ROWS, high - ROWS)
        return pltpu.make_async_remote_copy(
            src_ref=targets[array].at[pl.ds(origin, count)],
            dst_ref=targets[array].at[pl.ds(first, count)],
            send_sem=halo_send.at[index, side],
            recv_sem=halo_recv.at[index, side],
            device_id=(t, jnp.where(side == 0, s + 1, s - 1)),
            device_id_type=MESH,
        )

    far_to = 1 - core
    far_side = core
    far_valid = jnp.logical_not(is_first | is_last)

    @pl.when(far_valid)
    def _():
        for index in range(len(PIECES)):
            halo_copy(index, far_to).start()

    for index in range(len(PIECES)):
        halo_copy(index, 1 - far_to).start()

    greet(known.at[0], PASSES[0], -1)

    lane = lax.broadcasted_iota(jnp.int32, (8, LANES), 1)
    k_table = jnp.zeros((8, LANES), F32)
    n_table = jnp.zeros((8, LANES), F32)
    for i in range(k_ref.shape[0]):
        k_table = jnp.where(lane == i, k_ref[i], k_table)
        n_table = jnp.where(lane == i, n_ref[i], n_table)
    compact = lax.rem(2 * lane, LANES)
    zi = lax.broadcasted_iota(jnp.int32, (NZ, NY), 0)
    yi = lax.broadcasted_iota(jnp.int32, (NZ, NY), 1)
    czi = lax.broadcasted_iota(jnp.int32, (CZ, CY), 0)
    cyi = lax.broadcasted_iota(jnp.int32, (CZ, CY), 1)

    def take(value, index):
        return jnp.take_along_axis(value, index, axis=1)

    def look_up(row):
        k_parts, m_parts = [], []
        for z in range(0, NZ, 8):
            k_line, m_line = [], []
            for y in range(0, NY, LANES):
                soil_now = cx[row, z : z + 8, y : y + LANES]
                k = take(k_table, soil_now)
                n = take(n_table, soil_now)
                m = n - 1.0
                ax[row, z : z + 8, y : y + LANES] = (DENSITY * k) * n
                mx[row, z : z + 8, y : y + LANES] = m
                k_line.append(k)
                m_line.append(m)
            k_parts.append(jnp.concatenate(k_line, axis=1))
            m_parts.append(jnp.concatenate(m_line, axis=1))
        return jnp.concatenate(k_parts, axis=0), jnp.concatenate(m_parts, axis=0)

    sub = lax.broadcasted_iota(jnp.int32, (8, LANES), 0)
    compact_z = lax.rem(2 * sub, 8)

    def restrict(total):
        out = []
        for i in range(CY // LANES):
            halves = []
            for half in range(2):
                y = (2 * i + half) * LANES
                parts = []
                for z in range(0, NZ, 8):
                    value = total[z : z + 8, y : y + LANES]
                    value = value + pltpu.roll(value, 7, 0)
                    parts.append(jnp.take_along_axis(value, compact_z, axis=0))
                value = jnp.where(sub < 4, parts[0], parts[1])
                value = value + pltpu.roll(value, LANES - 1, 1)
                halves.append(take(value, compact))
            out.append(jnp.where(lane < LANES // 2, halves[0], halves[1]))
        return 0.125 * jnp.concatenate(out, axis=1)

    def fields(p):
        k_low, m_low = look_up(2 * p)
        k_high, m_high = look_up(2 * p + 1)
        coarse_k = restrict(k_low + k_high)
        coarse_m = restrict(m_low + m_high)
        dc[p] = restrict(dx[2 * p] + dx[2 * p + 1])
        ac[p] = (DENSITY * coarse_k) * (coarse_m + 1.0)
        mc[p] = coarse_m

    def restrict_start(p):
        rc[p] = restrict(u0[2 * p] + u0[2 * p + 1])

    def fine_row(src, dst, row, shift=0):
        outside = (is_first & (row < HALO)) | (is_last & (row >= HALO + ROWS))
        c, w, e = src[row], src[row - 1], src[row + 1]
        dst[row - shift] = update(
            c, w, e,
            shifted(c, 0, NZ, 1, zi), shifted(c, 0, NZ, -1, zi),
            shifted(c, 1, NY, 1, yi), shifted(c, 1, NY, -1, yi),
            dx[row], ax[row], mx[row], jnp.where(outside, 0.0, 0.6), 1.0,
        )

    def loop(first, last, function):
        def run(i, carry):
            function(i)
            return carry

        lax.fori_loop(first, last, run, 0)

    loop(2, 6, fields)
    loop(2, 6, restrict_start)
    loop(5, 11, functools.partial(fine_row, u0, u1))
    loop(6, 10, functools.partial(fine_row, u1, u2))
    loop(7, 9, functools.partial(fine_row, u2, u1))
    greeted(known.at[0], PASSES[0], -1)
    greet(known.at[1], PASSES[1])

    def diagonal(side, d):
        for k, (src, dst) in enumerate(((u0, u1), (u1, u2), (u2, u1), (u1, fine_out))):
            low = HALO - d + k
            fine_row(src, dst, jnp.where(side == 0, low, EXT - 1 - low), HALO if k == 3 else 0)

    def arrive(side, valid, *indices):
        @pl.when(valid)
        def _():
            for index in indices:
                halo_copy(index, side).wait_recv()

    def pair_of(side, p):
        return jnp.where(side == 0, p, EXT // 2 - 1 - p)

    def work_side(side, valid, after=(None, None, None)):
        def then(index):
            if after[index] is not None:
                after[index]()

        arrive(side, valid, 0)
        diagonal(side, 0)
        restrict_start(pair_of(side, 1))
        then(0)
        arrive(side, valid, 1, 2)
        look_up(jnp.where(side == 0, 3, 12))
        diagonal(side, 1)
        then(1)
        arrive(side, valid, 3, 4, 5)
        fields(pair_of(side, 1))
        diagonal(side, 2)
        restrict_start(pair_of(side, 0))
        then(2)
        arrive(side, valid, 6, 7)
        look_up(jnp.where(side == 0, 1, 14))
        diagonal(side, 3)

    def windows(first, second):
        def tiles(value):
            return [value[:, i * LANES : (i + 1) * LANES] for i in range(CY // LANES)]

        def roll(values, steps):
            return [pltpu.roll(value, steps % LANES, 1) for value in values]

        zero = jnp.zeros((CZ, LANES), F32)
        left = [roll(tiles(first), 16 - 32 * k) for k in range(4)]
        right = [roll(tiles(second), 80 - 32 * k) for k in range(4)]
        out = []
        for i in range(CY // LANES):
            for k in range(4):
                a, b = left[k][i], right[k][i]
                if k == 0:
                    a = jnp.where(lane < 16, left[k][i - 1] if i else zero, a)
                    b = jnp.where(lane < 80, right[k][i - 1] if i else zero, b)
                if k == 3:
                    last = i + 1 == CY // LANES
                    a = jnp.where(lane < 48, a, zero if last else left[k][i + 1])
                    b = jnp.where(lane < 112, b, zero if last else right[k][i + 1])
                out.append(jnp.where(lane < 64, a, b))
        return out

    def slot(source, to_half):
        return pl.ds(1 + 2 * (source - (HALF // 2) * to_half), 2)

    def to_half(other):
        return 1 - half if other else half

    def in_halo(groups):
        return jnp.where(half == 0, s >= HALF - groups, s < HALF + groups)

    def field_copy(side, other):
        return pltpu.make_async_remote_copy(
            src_ref=fwin.at[t + SLICES * side],
            dst_ref=fbuf.at[slot(s, to_half(other))],
            send_sem=f_send.at[side, other],
            recv_sem=f_recv.at[s],
            device_id=(t, host_of(to_half(other), side)),
            device_id_type=MESH,
        )

    def field_sends(action):
        for other in range(2):
            for side in range(2):
                if other:
                    wanted = in_halo(reach(0))
                else:
                    wanted = jnp.logical_not(is_host & (side == my_side))

                @pl.when(wanted)
                def _():
                    action(field_copy(side, other))

    def coarse_row(src, row):
        outside = (is_first & (row < 2)) | (is_last & (row >= 2 + CROWS))
        c, w, e = src[row], src[row - 1], src[row + 1]
        return update(
            c, w, e,
            shifted(c, 0, CZ, 1, czi), shifted(c, 0, CZ, -1, czi),
            shifted(c, 1, CY, 1, cyi), shifted(c, 1, CY, -1, cyi),
            dc[row], ac[row], mc[row], jnp.where(outside, 0.0, 0.3), 2.0,
        )

    def from_far(row, rows):
        return jnp.where(far_side == 0, row, rows - 1 - row)

    def own_first(r):
        row = from_far(r, EXT // 2)
        rc1[row] = coarse_row(rc, row)

    def own_second(r):
        row = from_far(r, EXT // 2)
        own[row - 2] = coarse_row(rc1, row)

    def make_drift(r):
        row = from_far(r, CROWS)
        now = restrict(fine_out[2 * row] + fine_out[2 * row + 1]) - own[row]
        drift[row] = now + jnp.where(t == 0, own[row], 0.0)

    def drift_windows(r):
        q = from_far(r, CROWS // 2)
        for j, value in enumerate(windows(drift[2 * q], drift[2 * q + 1])):
            win[j, q] = value

    def own_early():
        loop(2, 7, own_first)
        loop(3, 6, own_second)

    def own_late():
        own_first(1)
        own_second(2)

    work_side(1 - far_side, True)

    def field_windows(q):
        for which, ref in enumerate((dc, ac, mc)):
            for j, value in enumerate(windows(ref[2 + 2 * q], ref[3 + 2 * q])):
                fwin[j, q, which] = value

    loop(0, CROWS // 2, field_windows)

    @pl.when(is_host)
    def _():
        fbuf[slot(s, half)] = fwin[my_window]

    greeted(known.at[1], PASSES[1])
    greet(known.at[2], PASSES[2])

    def send_fields():
        @pl.when(far_valid)
        def _():
            for index in range(len(PIECES)):
                halo_copy(index, far_to).wait_send()

        greeted(known.at[2], PASSES[2])
        field_sends(lambda copy: copy.start())
        loop(1, CROWS, make_drift)
        drift_windows(1)

    work_side(far_side, far_valid, (own_early, send_fields, own_late))
    make_drift(0)
    drift_windows(0)

    def win_copy(j, other):
        return pltpu.make_async_remote_copy(
            src_ref=win.at[j],
            dst_ref=cbuf.at[t, slot(s, to_half(other))],
            send_sem=win_send.at[j, other],
            recv_sem=win_recv.at[t, s],
            device_id=(lax.rem(j, SLICES), host_of(to_half(other), j // SLICES)),
            device_id_type=MESH,
        )

    def win_sends(action):
        sends = t < SLICES - 1

        @pl.when(sends & in_halo((17 - 2 * t) // 4))
        def _():
            for j in range(WINDOWS):
                action(win_copy(j, 1))

        @pl.when(sends & jnp.logical_not(is_host))
        def _():
            for j in range(WINDOWS):
                action(win_copy(j, 0))

        @pl.when(sends & is_host)
        def _():
            for d in range(1, WINDOWS):
                action(win_copy(lax.rem(my_window + d, WINDOWS), 0))

    win_sends(lambda copy: copy.start())

    @pl.when(is_host & (t < SLICES - 1))
    def _():
        cbuf[t, slot(s, half)] = win[my_window]

    def result_copy(link, r):
        return pltpu.make_async_remote_copy(
            src_ref=gout.at[link, r],
            dst_ref=gbuf.at[my_window],
            send_sem=g_send.at[link, r],
            recv_sem=g_recv.at[my_window],
            device_id=(link + 1, HALF * half + r),
            device_id_type=MESH,
        )

    def result_sends(link, action):
        me = s - HALF * half

        @pl.when(t != link + 1)
        def _():
            action(result_copy(link, me))

        for d in range(1, HALF):
            action(result_copy(link, lax.rem(me + d, HALF)))

    @pl.when(is_host)
    def _():
        y = 32 * my_window - 16 + lax.rem(lane, 64)
        scale = jnp.where((y >= 0) & (y < CY), 0.3, 0.0)
        edge = jnp.zeros((1, CZ, LANES), F32)
        for row in (0, PACKED + 1):
            cbuf[0, row : row + 1] = edge

        def clear_row(row):
            cw0[row] = edge[0]
            cw1[row] = edge[0]

        loop(0, PACKED + 2, clear_row)

        def source(k):
            return jnp.where(half == 0, k, SPACE - 1 - k)

        for k in range(GROUPS):
            @pl.when(source(k) != s)
            def _():
                pltpu.make_async_remote_copy(
                    src_ref=fwin.at[0], dst_ref=fbuf.at[slot(source(k), half)], send_sem=f_send.at[0, 0],
                    recv_sem=f_recv.at[source(k)], device_id=(t, s + 1), device_id_type=MESH,
                ).wait_recv()

        def wait_slice(tau):
            def wait(device):
                pltpu.make_async_remote_copy(
                    src_ref=win.at[0], dst_ref=cbuf.at[tau, slot(device, half)],
                    send_sem=win_send.at[0, 0], recv_sem=win_recv.at[tau, device],
                    device_id=(t, s + 1), device_id_type=MESH,
                ).wait_recv()

            @pl.when(t != tau)
            def _():
                wait(s)

            for d in range(1, HALF):
                wait(HALF * half + lax.rem(s + d, HALF))
            for k in range(HALF, HALF + reach(tau)):
                wait(source(k))

        def block(src, first, count):
            u = src[pl.ds(first - 1, count + 2)]
            c = u[1 : count + 1]
            crossed = pltpu.roll(u, LANES // 2, 2)
            is_left = lax.broadcasted_iota(jnp.int32, (count, CZ, LANES), 2) < LANES // 2
            zs = lax.broadcasted_iota(jnp.int32, (count, CZ, LANES), 1)
            at = pl.ds(first, count)
            return update(
                c,
                jnp.where(is_left, crossed[:count], crossed[1 : count + 1]),
                jnp.where(is_left, crossed[1 : count + 1], crossed[2:]),
                jnp.where(zs == 0, 0.0, pltpu.roll(c, 1, 1)),
                jnp.where(zs == CZ - 1, 0.0, pltpu.roll(c, CZ - 1, 1)),
                pltpu.roll(c, 1, 2), pltpu.roll(c, LANES - 1, 2),
                fbuf[at, 0], fbuf[at, 1], fbuf[at, 2], scale, 2.0,
            )

        def condense(value):
            pairs = value.reshape(HALF, 2, CZ, LANES)
            a, b = pairs[:, 0], pairs[:, 1]
            at = lax.broadcasted_iota(jnp.int32, (HALF, CZ, LANES), 2) // 32
            front = jnp.where(at == 0, pltpu.roll(a, LANES - 16, 2), pltpu.roll(a, LANES - 48, 2))
            back = jnp.where(at == 2, pltpu.roll(b, 48, 2), pltpu.roll(b, 16, 2))
            return jnp.where(at < 2, front, back)

        first_own = 1 + (PACKED - OWN_PACKED) * half

        wait_slice(0)
        for link in range(SLICES - 1):
            src = cbuf.at[0] if link == 0 else cw0
            halo = (15 - (2 * link + 1)) // 2
            first = jnp.where(half == 0, 1 + OWN_PACKED, 1 + PACKED - OWN_PACKED - halo)
            cw1[pl.ds(first_own, OWN_PACKED)] = block(src, first_own, OWN_PACKED)
            if halo:
                cw1[pl.ds(first, halo)] = block(src, first, halo)
            last = link == SLICES - 2
            if not last:
                wait_slice(link + 1)
            value = block(cw1, first_own, OWN_PACKED)
            gout[link] = condense(value)
            result_sends(link, lambda copy: copy.start())

            @pl.when(t == link + 1)
            def _():
                gbuf[my_window] = gout[link, s - HALF * half]

            if not last:
                at = pl.ds(first_own, OWN_PACKED)
                cw0[at] = value + cbuf[link + 1, at]
            halo = (15 - (2 * link + 2)) // 2
            first = jnp.where(half == 0, 1 + OWN_PACKED, 1 + PACKED - OWN_PACKED - halo)
            if halo:
                at = pl.ds(first, halo)
                cw0[at] = block(cw1, first, halo) + cbuf[link + 1, at]

    @pl.when(t == 0)
    def _():
        diff_out[...] = own[...] - own[...]

    @pl.when(t > 0)
    def _():
        def wait_result(j):
            pltpu.make_async_remote_copy(
                src_ref=gout.at[0, 0], dst_ref=gbuf.at[j], send_sem=g_send.at[0, 0],
                recv_sem=g_recv.at[j], device_id=(t, s + 1 - 2 * core), device_id_type=MESH,
            ).wait_recv()

        @pl.when(is_host)
        def _():
            for d in range(1, WINDOWS):
                wait_result(lax.rem(my_window + d, WINDOWS))

        @pl.when(jnp.logical_not(is_host))
        def _():
            for j in range(WINDOWS):
                wait_result(j)

        quarter = lane // 32

        def assemble(row):
            for i in range(CY // LANES):
                value = jnp.zeros((CZ, LANES), F32)
                for k in range(4):
                    steps = 32 * (k - row) % LANES
                    value = jnp.where(quarter == k, pltpu.roll(gbuf[4 * i + k], steps, 1), value)
                where = slice(i * LANES, (i + 1) * LANES)
                diff_out[row, :, where] = value - own[row, :, where]

        for row in range(CROWS):
            assemble(row)

    for index in range(len(PIECES)):
        halo_copy(index, 1 - far_to).wait_send()

    field_sends(lambda copy: copy.wait_send())
    win_sends(lambda copy: copy.wait_send())

    @pl.when(is_host)
    def _():
        for link in range(SLICES - 1):
            result_sends(link, lambda copy: copy.wait_send())


def correct_kernel(fine, diff, out, result, sems):
    lane = lax.broadcasted_iota(jnp.int32, (CZ, LANES), 1)
    sub = lax.broadcasted_iota(jnp.int32, (CZ, LANES), 0)

    def copy(row):
        rows = pl.ds(2 * row, 2)
        return pltpu.make_async_copy(result.at[rows], out.at[rows], sems.at[row])

    for row in range(CROWS):
        for tile in range(NY // LANES):
            index = lane // 2 + (LANES // 2) * (tile % 2)
            source = diff[row, :, (tile // 2) * LANES : (tile // 2 + 1) * LANES]
            value = jnp.take_along_axis(source, index, axis=1)
            where = slice(tile * LANES, (tile + 1) * LANES)
            for half in range(2):
                wide = jnp.take_along_axis(value, sub // 2 + 4 * half, axis=0)
                for x in range(2):
                    at = (2 * row + x, slice(8 * half, 8 * half + 8), where)
                    result[at] = fine[at] + wide
        copy(row).start()
    for row in range(CROWS):
        copy(row).wait()


def body(start_states, dispersion, soil_class, sorption_k, sorption_n):
    vmem = pl.BlockSpec(memory_space=pltpu.VMEM)
    hbm = pl.BlockSpec(memory_space=pltpu.HBM)
    dma = pltpu.SemaphoreType.DMA
    grid = (EXT, NZ, NY)
    coarse = (EXT // 2, CZ, CY)
    tile = (CZ, LANES)
    scratch = [pltpu.SMEM((12,), F32) for _ in range(2)]
    scratch += [pltpu.VMEM(grid, F32) for _ in range(4)]
    scratch += [pltpu.VMEM(grid, jnp.int32)]
    scratch += [pltpu.VMEM(grid, F32) for _ in range(2)]
    scratch += [pltpu.VMEM(coarse, F32) for _ in range(2)]
    scratch += [pltpu.VMEM((CROWS, CZ, CY), F32)]
    scratch += [pltpu.VMEM(coarse, F32) for _ in range(3)]
    scratch += [pltpu.VMEM((CROWS, CZ, CY), F32)]
    scratch += [
        pltpu.VMEM((WINDOWS, CROWS // 2) + tile, F32),
        pltpu.VMEM((WINDOWS, CROWS // 2, 3) + tile, F32),
        pltpu.VMEM((SLICES - 1, PACKED + 2) + tile, F32),
        pltpu.VMEM((PACKED + 2, 3) + tile, F32),
        pltpu.VMEM((PACKED + 2,) + tile, F32),
        pltpu.VMEM((PACKED + 2,) + tile, F32),
        pltpu.VMEM((SLICES - 1, HALF) + tile, F32),
        pltpu.VMEM((WINDOWS,) + tile, F32),
        dma((5,)),
        dma((len(PIECES), 2)),
        dma((len(PIECES), 2)),
        dma((WINDOWS, 2)),
        dma((SLICES - 1, SPACE)),
        dma((2, 2)),
        dma((SPACE,)),
        dma((SLICES - 1, HALF)),
        dma((WINDOWS,)),
        pltpu.SemaphoreType.REGULAR((3,)),
    ]
    fine, diff = pl.pallas_call(
        main_kernel,
        out_shape=(
            pltpu.VMEM((ROWS, NZ, NY), F32),
            pltpu.VMEM((CROWS, CZ, CY), F32),
        ),
        in_specs=[hbm] * 5,
        out_specs=(vmem, vmem),
        scratch_shapes=scratch,
        compiler_params=pltpu.CompilerParams(
            collective_id=0, has_side_effects=True, vmem_limit_bytes=60 * 2**20
        ),
    )(sorption_k, sorption_n, start_states[0], dispersion, soil_class)
    out = pl.pallas_call(
        correct_kernel,
        out_shape=jax.ShapeDtypeStruct((ROWS, NZ, NY), F32),
        in_specs=[vmem, vmem],
        out_specs=hbm,
        scratch_shapes=[pltpu.VMEM((ROWS, NZ, NY), F32), dma((CROWS,))],
        compiler_params=pltpu.CompilerParams(vmem_limit_bytes=20 * 2**20),
    )(fine, diff)
    return out[None]


def solution(mesh):
    in_specs = (
        P("tm", "space", None, None),
        P("space", None, None),
        P("space", None, None),
        P(),
        P(),
    )
    out_specs = P("tm", "space", None, None)
    return jax.shard_map(body, mesh=mesh, in_specs=in_specs, out_specs=out_specs, check_vma=False)
```

profile of v0, /device:TPU:97, one launch (start us, length us, event | category | flops | bytes accessed | tf_op | source)
XLA Modules:
  0.0 32.7 jit_solution(10826782959095891941)
XLA Ops:
  0.0 31.8 %shard_map.55 = (f32[8,16,1024]{2,1,0:T(8,128)S(1)}, f32[4,8,512]{2,1,0:T(8,128)S(1)}) custom-call(f32[12]{0:T(128)} %k_in.1, f32[12]{0:T(128)} %n_in.1, f32[8,16,1024]{2,1,0:T(8,128)} %bitcast.2, f32[8,16,1024]{2,1,0:T(8,128)} %disp.1, s32[8,16,1024]{2,1,0:T(8,128)} %soil.1), custom_call_target="tpu_custom_call" | custom-call | tf_op jit(solution)/shard_map/pallas_call | solution.py:684
  31.8 0.9 %shard_map.56 = f32[8,16,1024]{2,1,0:T(8,128)} custom-call(f32[8,16,1024]{2,1,0:T(8,128)S(1)} %get-tuple-element.7.fine, f32[4,8,512]{2,1,0:T(8,128)S(1)} %get-tuple-element.8.diff), custom_call_target="tpu_custom_call" | custom-call | tf_op jit(solution)/shard_map/pallas_call | solution.py:697
where the time goes:
time: 32.9 us; the launch traced here: 32.7 us
  Pallas kernels  32.7 us (99%)
    pallas_call x1, Pallas kernels, body(): pl.pallas_call(main_kernel, out_shape=(pltpu.VMEM((ROWS, NZ, NY), F32), p...  31.8 us
    pallas_call x1, Pallas kernels, body(): pl.pallas_call(correct_kernel, out_shape=jax.ShapeDtypeStruct((ROWS, NZ,...  0.91 us

commit v1 on v0

--- a/solution.py
+++ b/solution.py
@@ -13,6 +13,7 @@
 SPEED_X = 0.3
 SPEED_Z = 0.2
 DENSITY = 2.0
+LOG2_E = 1.4426950408889634
 
 ROWS = 8
 HALO = 4
@@ -62,8 +63,8 @@
 def update(c, w, e, zm, zp, ym, yp, d, a, m, scale, per_h):
     lap = ((w + e) + (zm + zp)) + ((ym + yp) - 6.0 * c)
     adv = (SPEED_X * per_h) * (c - w) + (SPEED_Z * per_h) * (c - zm)
-    ret = 1.0 + a * jnp.exp(m * jnp.log(jnp.abs(c) + 0.1))
-    return c + scale * ((d * lap - adv) / ret)
+    ret = 1.0 + a * jnp.exp2(m * jnp.log(jnp.abs(c) + 0.1))
+    return c + (scale * (d * lap - adv)) * pl.reciprocal(ret, approx=True)
 
 
 def main_kernel(
@@ -198,7 +199,7 @@
                 n = take(n_table, soil_now)
                 m = n - 1.0
                 ax[row, z : z + 8, y : y + LANES] = (DENSITY * k) * n
-                mx[row, z : z + 8, y : y + LANES] = m
+                mx[row, z : z + 8, y : y + LANES] = LOG2_E * m
                 k_line.append(k)
                 m_line.append(m)
             k_parts.append(jnp.concatenate(k_line, axis=1))
@@ -232,7 +233,7 @@
         coarse_m = restrict(m_low + m_high)
         dc[p] = restrict(dx[2 * p] + dx[2 * p + 1])
         ac[p] = (DENSITY * coarse_k) * (coarse_m + 1.0)
-        mc[p] = coarse_m
+        mc[p] = LOG2_E * coarse_m
 
     def restrict_start(p):
         rc[p] = restrict(u0[2 * p] + u0[2 * p + 1])

time: 32.9 us -> 32.9 us (level)
  no operation moved by 1% of the time
where the time goes in v1:
time: 32.9 us; the launch traced here: 32.7 us
  Pallas kernels  32.7 us (99%)
    pallas_call x1, Pallas kernels, body(): pl.pallas_call(main_kernel, out_shape=(pltpu.VMEM((ROWS, NZ, NY), F32), p...  31.8 us
    pallas_call x1, Pallas kernels, body(): pl.pallas_call(correct_kernel, out_shape=jax.ShapeDtypeStruct((ROWS, NZ,...  0.91 us

profile of v1, /device:TPU:97, one launch (start us, length us, event | category | flops | bytes accessed | tf_op | source)
XLA Modules:
  0.0 32.7 jit_solution(7666115794062892377)
XLA Ops:
  0.0 31.8 %shard_map.55 = (f32[8,16,1024]{2,1,0:T(8,128)S(1)}, f32[4,8,512]{2,1,0:T(8,128)S(1)}) custom-call(f32[12]{0:T(128)} %k_in.1, f32[12]{0:T(128)} %n_in.1, f32[8,16,1024]{2,1,0:T(8,128)} %bitcast.2, f32[8,16,1024]{2,1,0:T(8,128)} %disp.1, s32[8,16,1024]{2,1,0:T(8,128)} %soil.1), custom_call_target="tpu_custom_call" | custom-call | tf_op jit(solution)/shard_map/pallas_call | solution.py:685
  31.8 0.9 %shard_map.56 = f32[8,16,1024]{2,1,0:T(8,128)} custom-call(f32[8,16,1024]{2,1,0:T(8,128)S(1)} %get-tuple-element.7.fine, f32[4,8,512]{2,1,0:T(8,128)S(1)} %get-tuple-element.8.diff), custom_call_target="tpu_custom_call" | custom-call | tf_op jit(solution)/shard_map/pallas_call | solution.py:698
